TPU v7x, 32 devices: a whole 2x2x4 slice. The times are simulated.
32 devices in a mesh: aux: 2 (over core), occ: 16 (over z, y, x).
Axes of the slice: x: 2, y: 2, z: 4, core: 2. Of those that a mesh axis runs over, the one named last changes fastest.
Arguments:
- factors: float32 [2048, 16, 512], P('aux', 'occ'), may hold values from -0.3 to 0.3
- eps_occ: float32 [16], P('occ'), may hold values from -2 to -0.3
- eps_virt: float32 [512], replicated, may hold values from 0.2 to 3
- pair_mask: int32 [16, 4], P('occ'), may hold values 0 or 1
Outputs:
- gradient: float32 [2048, 16, 512], P('aux', 'occ')
Inputs may be any that keep to these rules, and one draw needn't show every extreme that they name: `pair_mask`: 1 marks a surviving pair.
All inputs are finite; a program needn't handle non-finite values. No bound on the sum of `pair_mask` on one device may be relied on, other than what follows from the above.
Results may differ from a plain program's by a relative error of at most 0.0003.
Values sent between devices are 32-bit elements; how exact they have to be, the bound alone decides.
No kernel may reach another device: no remote copies, remote signals or barrier semaphores. Data moves between devices by JAX's collectives and lax.ppermute only.
A program may use at most 128 MiB of HBM per device.

v0:
```python
import functools

import jax
import jax.numpy as jnp
from jax import lax
from jax.experimental import pallas as pl
from jax.experimental.pallas import tpu as pltpu
from jax.sharding import PartitionSpec as P

LANES = 128
SUBLANES = 8
PLANE = 4
CHUNKS = 4
VMEM_LIMIT = 60 * 1024 * 1024


def split(value):
    high = value.astype(jnp.bfloat16)
    low = (value - high.astype(jnp.float32)).astype(jnp.bfloat16)
    return high, low


def deep_left(value):
    high, low = split(value)
    return jnp.concatenate([high, low, high], axis=1)


def deep_right(value):
    high, low = split(value)
    return jnp.concatenate([high, high, low], axis=0)


def dot(left, right):
    numbers = (((1,), (0,)), ((), ()))
    return lax.dot_general(left, right, numbers, preferred_element_type=jnp.float32)


def rows_of(ref, start, count, width):
    lines = width // LANES
    columns = [ref[pl.ds(start * lines + at, count, stride=lines), :] for at in range(lines)]
    return jnp.concatenate(columns, axis=1)


def distinct(arrays):
    return list({id(array): array for array in arrays}.values())


class Copies:
    def __init__(self, semaphores):
        self.semaphores = semaphores
        self.used = 0

    def start(self, source, target):
        copy = pltpu.make_async_copy(source, target, self.semaphores.at[self.used])
        self.used += 1
        copy.start()
        return copy


def call(kernel, smem, vmem, anywhere, outputs, out_space, scratch, flops):
    spaces = [pltpu.SMEM] * len(smem) + [pltpu.VMEM] * len(vmem) + [pl.ANY] * len(anywhere)
    moved = sum(a.size * a.dtype.itemsize for a in (*vmem, *anywhere, *outputs))
    return pl.pallas_call(
        kernel,
        out_shape=outputs,
        in_specs=[pl.BlockSpec(memory_space=space) for space in spaces],
        out_specs=[pl.BlockSpec(memory_space=out_space)] * len(outputs),
        scratch_shapes=scratch,
        compiler_params=pltpu.CompilerParams(vmem_limit_bytes=VMEM_LIMIT),
        cost_estimate=pl.CostEstimate(flops=flops, bytes_accessed=moved, transcendentals=0),
    )(*smem, *vmem, *anywhere)


def prepare(own, rows, width):
    size = rows // CHUNKS
    cut = size * width // LANES

    def kernel(own_ref, high_ref, low_ref, integrals_ref, block_ref, semaphores):
        copies = Copies(semaphores)
        coming = [copies.start(own_ref.at[pl.ds(at * cut, cut)], block_ref.at[at]) for at in range(CHUNKS)]
        for at in range(CHUNKS):
            coming[at].wait()
            block = rows_of(block_ref.at[at], 0, size, width)
            high, low = split(block.T)
            high_ref[at] = high
            low_ref[at] = low
            value = dot(jnp.concatenate([high, low, high], axis=1), deep_right(block))
            integrals_ref[...] = integrals_ref[...] + value if at else value

    half = jax.ShapeDtypeStruct((CHUNKS, width, size), jnp.bfloat16)
    square = jax.ShapeDtypeStruct((width, width), jnp.float32)
    scratch = [pltpu.VMEM((CHUNKS, cut, LANES), jnp.float32), pltpu.SemaphoreType.DMA((CHUNKS,))]
    flops = 6 * rows * width * width
    return call(kernel, [], [], [own], [half, half, square], pltpu.VMEM, scratch, flops)


def integrate(turned, slots, first, size, width, before=()):
    cut = size * width // LANES
    count = len(slots)
    pieces = [piece for slot in slots for piece in slot]
    arrays = distinct([array for array, _ in pieces])
    numbers = [list(range(start, start + len(slot))) for slot, start in zip(slots, first)]
    needed = sorted({number for some in numbers for number in some})
    before = list(before)

    def kernel(*refs):
        given = iter(refs)
        high_ref, low_ref = next(given), next(given)
        before_refs = [next(given) for _ in before]
        ref_of = {id(array): next(given) for array in arrays}
        outs = [next(given) for _ in range(count)]
        turned_ref, block_ref, before_ref, semaphores = given
        copies = Copies(semaphores)
        coming, turning = [], {}

        def turn(number):
            if number not in turning:
                at = needed.index(number)
                turning[number] = [
                    copies.start(high_ref.at[number], turned_ref.at[at, 0]),
                    copies.start(low_ref.at[number], turned_ref.at[at, 1]),
                ]

        at = 0
        for slot in range(count):
            for number, (array, base) in zip(numbers[slot], slots[slot]):
                turn(number)
                coming.append(copies.start(ref_of[id(array)].at[pl.ds(base, cut)], block_ref.at[at]))
                at += 1
        adding = [copies.start(ref, before_ref.at[slot]) for slot, ref in enumerate(before_refs)]
        at = 0
        for slot in range(count):
            for place, number in enumerate(numbers[slot]):
                for copy in turning.pop(number, []):
                    copy.wait()
                coming[at].wait()
                there = needed.index(number)
                high, low = turned_ref[there, 0], turned_ref[there, 1]
                left = jnp.concatenate([high, low, high], axis=1)
                value = dot(left, deep_right(rows_of(block_ref.at[at], 0, size, width)))
                outs[slot][...] = outs[slot][...] + value if place else value
                at += 1
            if before:
                adding[slot].wait()
                outs[slot][...] += before_ref[slot]

    out = [jax.ShapeDtypeStruct((width, width), jnp.float32)] * count
    scratch = [
        pltpu.VMEM((len(needed), 2, width, size), jnp.bfloat16),
        pltpu.VMEM((len(pieces), cut, LANES), jnp.float32),
        pltpu.VMEM((max(len(before), 1), width, width), jnp.float32),
        pltpu.SemaphoreType.DMA((2 * len(needed) + len(pieces) + len(before),)),
    ]
    flops = 6 * len(pieces) * size * width * width
    return call(kernel, [], [], [*turned, *before, *arrays], out, pltpu.VMEM, scratch, flops)


def contract(partials, slots, signs, energies, eps_virt, size, before=None):
    count = len(slots)
    chunks = len(slots[0])
    virt = eps_virt.shape[1]
    width = partials[0][0].shape[0]
    occ_rows = width // virt
    lines = width // LANES
    cut = size * lines
    sums = [array for slot in partials for array in slot]
    pieces = [piece for slot in slots for piece in slot]
    arrays = distinct([array for array, _ in (*pieces, *energies)])
    last = [before] if before is not None else []

    def kernel(*refs):
        given = iter(refs)
        sign_ref, virt_ref = next(given), next(given)
        sum_refs = [next(given) for _ in sums]
        before_refs = [next(given) for _ in last]
        ref_of = {id(array): next(given) for array in arrays}
        out_ref, energy_ref, sum_ref, block_ref, result_ref, right_ref, semaphores = given
        copies = Copies(semaphores)
        arriving = [
            copies.start(ref_of[id(array)].at[pl.ds(base, SUBLANES)], energy_ref.at[at])
            for at, (array, base) in enumerate(energies)
        ]
        arriving += [copies.start(ref, sum_ref.at[at]) for at, ref in enumerate(sum_refs)]
        coming = [
            [
                copies.start(ref_of[id(slots[slot][at][0])].at[pl.ds(slots[slot][at][1], cut)], block_ref.at[slot, at])
                for slot in range(count)
            ]
            for at in range(chunks)
        ]
        adding = [
            [copies.start(ref.at[pl.ds(at * cut, cut)], result_ref.at[at]) for ref in before_refs]
            for at in range(chunks)
        ]
        for copy in arriving:
            copy.wait()

        def line(at):
            virtual = virt_ref[...]
            energy = energy_ref[at]
            return jnp.concatenate([virtual - energy[:1, i : i + 1] for i in range(occ_rows)], axis=1)

        row = jnp.broadcast_to(line(0), (SUBLANES, width)).T[:, :1]
        at = 0
        for slot in range(count):
            total = sum_ref[at]
            for extra in range(1, len(partials[slot])):
                total = total + sum_ref[at + extra]
            at += len(partials[slot])
            amplitude = (sign_ref[slot] * total) / (row + line(slot + 1))
            right_ref[pl.ds(slot * 3 * width, 3 * width), :] = deep_right(amplitude.T)
        leaving = []
        for at in range(chunks):
            for copy in coming[at] + adding[at]:
                copy.wait()
            left = [deep_left(rows_of(block_ref.at[slot, at], 0, size, width)) for slot in range(count)]
            value = dot(jnp.concatenate(left, axis=1), right_ref[...])
            for column in range(lines):
                lanes = value[:, column * LANES : (column + 1) * LANES]
                where = pl.ds(column, size, stride=lines)
                if last:
                    lanes = lanes + result_ref[at, where, :]
                result_ref[at, where, :] = lanes
            leaving.append(copies.start(result_ref.at[at], out_ref.at[pl.ds(at * cut, cut)]))
        for copy in leaving:
            copy.wait()

    rows = chunks * size
    out = jax.ShapeDtypeStruct((rows * lines, LANES), jnp.float32)
    scratch = [
        pltpu.VMEM((len(energies), SUBLANES, LANES), jnp.float32),
        pltpu.VMEM((len(sums), width, width), jnp.float32),
        pltpu.VMEM((count, chunks, cut, LANES), jnp.float32),
        pltpu.VMEM((chunks, cut, LANES), jnp.float32),
        pltpu.VMEM((count * 3 * width, width), jnp.bfloat16),
        pltpu.SemaphoreType.DMA((len(energies) + len(sums) + len(pieces) + 2 * chunks,)),
    ]
    flops = 6 * count * rows * width * width
    return call(kernel, [signs], [eps_virt], [*sums, *last, *arrays], [out], pl.ANY, scratch, flops)[0]


def after(block, *others):
    return lax.optimization_barrier((block, *others))[0]


def on_device(factors, eps_occ, eps_virt, pair_mask):
    rows, occ_rows, virt = factors.shape
    width = occ_rows * virt
    lines = width // LANES
    groups = lax.axis_size("occ")
    shares = lax.axis_size("aux")
    size = rows // CHUNKS
    cut = size * lines
    last = CHUNKS - 1
    group = lax.axis_index("occ")
    place = group % PLANE
    odd_x = place % 2 == 1
    odd_y = place // 2 == 1

    own = factors.reshape(rows * lines, LANES)
    energies = jnp.zeros((SUBLANES * LANES,), jnp.float32).at[:occ_rows].set(eps_occ)
    energies = energies.reshape(SUBLANES, LANES)

    def part(whole, at):
        return whole[at * cut : (at + 1) * cut]

    def swap(block, bit):
        return lax.ppermute(block, "occ", [(g, g ^ bit) for g in range(groups)])

    def up(block):
        return lax.ppermute(block, "occ", [(g, g + PLANE) for g in range(groups - PLANE)])

    def totals(partial):
        if shares == 2:
            return [partial, lax.ppermute(partial, "aux", [(0, 1), (1, 0)])]
        return [lax.psum(partial, "aux")]

    def sign(offset):
        flag = lax.dynamic_index_in_dim(pair_mask[0], offset - 1, 0, keepdims=False)
        return jnp.where((group >= offset) & (flag > 0), -1.0, 0.0).astype(jnp.float32)

    sign_own = jnp.float32(-1.0)
    sign_z = sign(jnp.int32(PLANE))
    sign_x = sign(jnp.where(odd_x, 1, PLANE - 1))
    sign_y = sign(jnp.int32(PLANE // 2))
    sign_d = sign(jnp.where(odd_x, PLANE - 1, 1))

    first_sent = jnp.concatenate([part(own, 0), energies])

    def add(partials, slots, signs, carriers, before=None):
        where = [(first_sent, cut)] + [(carrier, cut) for carrier in carriers]
        return contract(partials, slots, jnp.stack(signs), where, eps_virt[None, :], size, before)

    from_z, from_x, from_y, from_d = [], [], [], []
    from_z.append(up(first_sent))
    high, low, partial_own = prepare(own, rows, width)
    turned = (high, low)
    sums_own = totals(partial_own)
    def slot_of(blocks):
        return [(block, 0) for block in blocks]

    slot_own = [(own, at * cut) for at in range(CHUNKS)]
    ready = [partial_own]
    for at in range(CHUNKS):
        mine, came = lax.optimization_barrier((own, from_z[at]))
        mine = part(mine, at) if at else first_sent
        send_x = after(jnp.where(odd_x, came, mine), *ready)
        send_y = jnp.where(odd_y, came, mine)
        from_x.append(swap(send_x, 1))
        from_y.append(swap(send_y, 2))
        if at < last:
            from_z.append(up(part(after(own, from_z[at], partial_own), at + 1)))
        ready = [from_x[at]]
        from_d.append(swap(after(from_y[at], from_d[at - 1] if at else from_x[0]), 1))

    slot_z, slot_x, slot_y, slot_d = map(slot_of, (from_z, from_x, from_y, from_d))
    partial_z, partial_y = integrate(after(turned, from_x[2]), [slot_z, slot_y], [0, 0], size, width)
    gradient = add(
        [sums_own, totals(partial_z), totals(partial_y)], [slot_own, slot_z, slot_y],
        [sign_own, sign_z, sign_y], [first_sent, from_z[0], from_y[0]],
    )
    turned = after(turned, gradient)
    early = integrate(turned, [slot_x[:last], slot_d[: last - 1]], [0, 0], size, width)
    partial_x, partial_d = integrate(
        turned, [slot_x[last:], slot_d[last - 1 : last]], [last, last - 1], size, width, early
    )
    (partial_d,) = integrate(turned, [slot_d[last:]], [last], size, width, [partial_d])
    gradient = add(
        [totals(partial_x), totals(partial_d)], [slot_x, slot_d],
        [sign_x, sign_d], [from_x[0], from_d[0]], gradient,
    )
    return gradient.reshape(rows, occ_rows, virt)


def solution(mesh):
    if mesh.shape["occ"] % PLANE:
        raise ValueError("incomplete plane")
    in_specs = (P("aux", "occ", None), P("occ"), P(), P("occ", None))
    out_specs = P("aux", "occ", None)
    return jax.shard_map(
        on_device, mesh=mesh, in_specs=in_specs, out_specs=out_specs, check_vma=False
    )
```

profile of v0, /device:TPU:0, one launch (start us, length us, event | category | flops | bytes accessed | tf_op | source)
XLA Modules:
  0.0 147.5 jit_solution(18238830216914541363)
XLA Ops:
  2.1 5.7 %collective-permute-start.1 = (f32[1032,128]{1,0:T(8,128)S(1)}, f32[1032,128]{1,0:T(8,128)}, u32[]{:S(2)}, u32[]{:S(2)}) collective-permute-start(f32[1032,128]{1,0:T(8,128)S(1)} %pad_maximum_fusion.refs_17_.refs_15_), channel_id=1, source_target_pairs={{0,4},{1,5},{2,6},{3,7},{4,8},{5,9},{6,10},{7,11},{8,12},{9,13},{1... | collective-permute-start | bytes 1585160 | tf_op jit(solution)/shard_map/ppermute | solution.py:271
  7.9 4.7 %shard_map.46 = (bf16[4,512,256]{2,1,0:T(8,128)(2,1)}, bf16[4,512,256]{2,1,0:T(8,128)(2,1)}, f32[512,512]{1,0:T(8,128)}) custom-call(f32[4096,128]{1,0:T(8,128)} %bitcast.14), custom_call_target="tpu_custom_call" | custom-call | flops 1610612736 | bytes 5242880 | tf_op jit(solution)/shard_map/pallas_call | solution.py:63
  12.5 5.8 %collective-permute-done.1.refs_2_.refs_9_ = f32[1032,128]{1,0:T(8,128)} collective-permute-done((f32[1032,128]{1,0:T(8,128)S(1)}, f32[1032,128]{1,0:T(8,128)}, u32[]{:S(2)}, u32[]{:S(2)}) %collective-permute-start.1) | collective-permute-done | bytes 528416 | tf_op jit(solution)/shard_map/ppermute | solution.py:271
  18.4 4.5 %collective-permute-start.2 = (f32[1024,128]{1,0:T(8,128)S(1)}, f32[1024,128]{1,0:T(8,128)S(1)}, u32[]{:S(2)}, u32[]{:S(2)}) collective-permute-start(f32[1024,128]{1,0:T(8,128)S(1)} %slice.39), channel_id=1, source_target_pairs={{0,4},{1,5},{2,6},{3,7},{4,8},{5,9},{6,10},{7,11},{8,12},{9,13},{1... | collective-permute-start | bytes 1572872 | tf_op jit(solution)/shard_map/ppermute | solution.py:271
  25.6 7.6 %collective-permute-done.2.refs_3_.refs_10_ = f32[1024,128]{1,0:T(8,128)S(1)} collective-permute-done((f32[1024,128]{1,0:T(8,128)S(1)}, f32[1024,128]{1,0:T(8,128)S(1)}, u32[]{:S(2)}, u32[]{:S(2)}) %collective-permute-start.2) | collective-permute-done | bytes 524320 | tf_op jit(solution)/shard_map/ppermute | solution.py:271
  33.2 4.4 %collective-permute-start.3 = (f32[1024,128]{1,0:T(8,128)S(1)}, f32[1024,128]{1,0:T(8,128)S(1)}, u32[]{:S(2)}, u32[]{:S(2)}) collective-permute-start(f32[1024,128]{1,0:T(8,128)S(1)} %slice.40), channel_id=1, source_target_pairs={{0,4},{1,5},{2,6},{3,7},{4,8},{5,9},{6,10},{7,11},{8,12},{9,13},{1... | collective-permute-start | bytes 1572872 | tf_op jit(solution)/shard_map/ppermute | solution.py:271
  37.6 1.6 %collective-permute-start.8 = (f32[1032,128]{1,0:T(8,128)S(1)}, f32[1032,128]{1,0:T(8,128)S(1)}, u32[]{:S(2)}, u32[]{:S(2)}) collective-permute-start(f32[1032,128]{1,0:T(8,128)S(1)} %get-tuple-element.85), channel_id=1, source_target_pairs={{0,2},{1,3},{2,0},{3,1},{4,6},{5,7},{6,4},{7,5},{8,10},{9,11},{10,... | collective-permute-start | bytes 1585160 | tf_op jit(solution)/shard_map/ppermute | solution.py:268
  39.3 1.6 %collective-permute-start.5 = (f32[1024,128]{1,0:T(8,128)S(1)}, f32[1024,128]{1,0:T(8,128)S(1)}, u32[]{:S(2)}, u32[]{:S(2)}) collective-permute-start(f32[1024,128]{1,0:T(8,128)S(1)} %get-tuple-element.59), channel_id=1, source_target_pairs={{0,1},{1,0},{2,3},{3,2},{4,5},{5,4},{6,7},{7,6},{8,9},{9,8},{10,11... | collective-permute-start | bytes 1572872 | tf_op jit(solution)/shard_map/ppermute | solution.py:268
  40.9 6.1 %collective-permute-done.3.refs_4_.refs_11_ = f32[1024,128]{1,0:T(8,128)S(1)} collective-permute-done((f32[1024,128]{1,0:T(8,128)S(1)}, f32[1024,128]{1,0:T(8,128)S(1)}, u32[]{:S(2)}, u32[]{:S(2)}) %collective-permute-start.3) | collective-permute-done | bytes 524320 | tf_op jit(solution)/shard_map/ppermute | solution.py:271
  47.0 4.6 %collective-permute-start.7 = (f32[1024,128]{1,0:T(8,128)S(1)}, f32[1024,128]{1,0:T(8,128)S(1)}, u32[]{:S(2)}, u32[]{:S(2)}) collective-permute-start(f32[1024,128]{1,0:T(8,128)S(1)} %slice.43), channel_id=1, source_target_pairs={{0,4},{1,5},{2,6},{3,7},{4,8},{5,9},{6,10},{7,11},{8,12},{9,13},{1... | collective-permute-start | bytes 1572872 | tf_op jit(solution)/shard_map/ppermute | solution.py:271
  51.6 1.6 %collective-permute-start.9 = (f32[1024,128]{1,0:T(8,128)S(1)}, f32[1024,128]{1,0:T(8,128)S(1)}, u32[]{:S(2)}, u32[]{:S(2)}) collective-permute-start(f32[1024,128]{1,0:T(8,128)S(1)} %get-tuple-element.83), channel_id=1, source_target_pairs={{0,2},{1,3},{2,0},{3,1},{4,6},{5,7},{6,4},{7,5},{8,10},{9,11},{10,... | collective-permute-start | bytes 1572872 | tf_op jit(solution)/shard_map/ppermute | solution.py:268
  55.9 4.0 %collective-permute-done.7.refs_5_.refs_12_ = f32[1024,128]{1,0:T(8,128)S(1)} collective-permute-done((f32[1024,128]{1,0:T(8,128)S(1)}, f32[1024,128]{1,0:T(8,128)S(1)}, u32[]{:S(2)}, u32[]{:S(2)}) %collective-permute-start.7) | collective-permute-done | bytes 524320 | tf_op jit(solution)/shard_map/ppermute | solution.py:271
  60.8 1.6 %collective-permute-start.11 = (f32[1024,128]{1,0:T(8,128)S(1)}, f32[1024,128]{1,0:T(8,128)S(1)}, u32[]{:S(2)}, u32[]{:S(2)}) collective-permute-start(f32[1024,128]{1,0:T(8,128)S(1)} %get-tuple-element.80), channel_id=1, source_target_pairs={{0,2},{1,3},{2,0},{3,1},{4,6},{5,7},{6,4},{7,5},{8,10},{9,11},{10,... | collective-permute-start | bytes 1572872 | tf_op jit(solution)/shard_map/ppermute | solution.py:268
  62.4 4.2 %collective-permute-done.9.refs_7_.refs_14_ = f32[1024,128]{1,0:T(8,128)S(1)} collective-permute-done((f32[1024,128]{1,0:T(8,128)S(1)}, f32[1024,128]{1,0:T(8,128)S(1)}, u32[]{:S(2)}, u32[]{:S(2)}) %collective-permute-start.9) | collective-permute-done | bytes 524320 | tf_op jit(solution)/shard_map/ppermute | solution.py:268
  66.5 1.7 %collective-permute-done.14.refs_5_.refs_11_ = f32[1032,128]{1,0:T(8,128)} collective-permute-done((f32[1032,128]{1,0:T(8,128)S(1)}, f32[1032,128]{1,0:T(8,128)}, u32[]{:S(2)}, u32[]{:S(2)}) %collective-permute-start.14) | collective-permute-done | bytes 528416 | tf_op jit(solution)/shard_map/ppermute | solution.py:268
  69.7 9.7 %collective-permute-done.6.refs_4_.refs_9_ = f32[1024,128]{1,0:T(8,128)} collective-permute-done((f32[1024,128]{1,0:T(8,128)S(1)}, f32[1024,128]{1,0:T(8,128)}, u32[]{:S(2)}, u32[]{:S(2)}) %collective-permute-start.6) | collective-permute-done | bytes 524320 | tf_op jit(solution)/shard_map/ppermute | solution.py:268
  80.3 4.5 %collective-permute-done.11.refs_9_.refs_16_ = f32[1024,128]{1,0:T(8,128)S(1)} collective-permute-done((f32[1024,128]{1,0:T(8,128)S(1)}, f32[1024,128]{1,0:T(8,128)S(1)}, u32[]{:S(2)}, u32[]{:S(2)}) %collective-permute-start.11) | collective-permute-done | bytes 524320 | tf_op jit(solution)/shard_map/ppermute | solution.py:268
  85.6 6.3 %shard_map.47 = (f32[512,512]{1,0:T(8,128)}, f32[512,512]{1,0:T(8,128)}) custom-call(bf16[4,512,256]{2,1,0:T(8,128)(2,1)} %get-tuple-element.68.refs_0_, bf16[4,512,256]{2,1,0:T(8,128)(2,1)} %get-tuple-element.69.refs_1_, f32[1032,128]{1,0:T(8,128)} %collective-permute-done.1.refs_2_.refs_9_, f32[1024,128]{1,0:T(8,128)} %copy-done.10, ...), custom_call_target="tpu_custom_call" | custom-call | flops 3221225472 | bytes 8396800 | tf_op jit(solution)/shard_map/pallas_call | solution.py:63
  97.2 10.2 %collective-permute-done.17.refs_5_.refs_13_ = f32[1024,128]{1,0:T(8,128)S(1)} collective-permute-done((f32[1024,128]{1,0:T(8,128)S(1)}, f32[1024,128]{1,0:T(8,128)S(1)}, u32[]{:S(2)}, u32[]{:S(2)}) %collective-permute-start.17) | collective-permute-done | bytes 524320 | tf_op jit(solution)/shard_map/ppermute | solution.py:268
  108.9 11.3 %shard_map.48.refs_6_ = f32[4096,128]{1,0:T(8,128)} custom-call(f32[3]{0:T(128)} %pad_maximum_fusion.2.refs_0_, f32[1,512]{1,0:T(1,128)} %bitcast.24, f32[512,512]{1,0:T(8,128)} %get-tuple-element.50.refs_2_, f32[512,512]{1,0:T(8,128)} %collective-permute-done.refs_3_, f32[512,512]{1,0:T(8,128)} %get-tuple-element.66.refs_4_, ...), custom_call_target="tpu_custom_call" | custom-call | flops 4831838208 | bytes 15218688 | tf_op jit(solution)/shard_map/pallas_call | solution.py:63
  120.2 4.8 %shard_map.49 = (f32[512,512]{1,0:T(8,128)}, f32[512,512]{1,0:T(8,128)}) custom-call(bf16[4,512,256]{2,1,0:T(8,128)(2,1)} %get-tuple-element.68.refs_0_, bf16[4,512,256]{2,1,0:T(8,128)(2,1)} %get-tuple-element.69.refs_1_, f32[1032,128]{1,0:T(8,128)} %copy-done.7, f32[1024,128]{1,0:T(8,128)} %copy-done.8, f32[1024,128]{1,0:T(8,128)} %collective-permute-done.6.refs_4_.refs_9_, ...), custom_call_target="tpu_custom_call" | custom-call | flops 2013265920 | bytes 6823936 | tf_op jit(solution)/shard_map/pallas_call | solution.py:63
  125.8 3.9 %shard_map.50 = (f32[512,512]{1,0:T(8,128)}, f32[512,512]{1,0:T(8,128)}) custom-call(bf16[4,512,256]{2,1,0:T(8,128)(2,1)} %get-tuple-element.68.refs_0_, bf16[4,512,256]{2,1,0:T(8,128)(2,1)} %get-tuple-element.69.refs_1_, f32[512,512]{1,0:T(8,128)} %get-tuple-element.72.refs_2_, f32[512,512]{1,0:T(8,128)} %get-tuple-element.73.refs_3_, ...), custom_call_target="tpu_custom_call" | custom-call | flops 805306368 | bytes 7340032 | tf_op jit(solution)/shard_map/pallas_call | solution.py:63
  130.7 3.1 %shard_map.51.refs_4_ = f32[512,512]{1,0:T(8,128)} custom-call(bf16[4,512,256]{2,1,0:T(8,128)(2,1)} %get-tuple-element.68.refs_0_, bf16[4,512,256]{2,1,0:T(8,128)(2,1)} %get-tuple-element.69.refs_1_, f32[512,512]{1,0:T(8,128)} %get-tuple-element.77.refs_2_, f32[1024,128]{1,0:T(8,128)} %copy-done.4), custom_call_target="tpu_custom_call" | custom-call | flops 402653184 | bytes 4718592 | tf_op jit(solution)/shard_map/pallas_call | solution.py:63
  138.0 9.2 %shard_map.52 = f32[4096,128]{1,0:T(8,128)} custom-call(f32[2]{0:T(128)} %pad_maximum_fusion.1.refs_0_, f32[1,512]{1,0:T(1,128)} %bitcast.25, f32[512,512]{1,0:T(8,128)} %get-tuple-element.76.refs_2_, f32[512,512]{1,0:T(8,128)} %copy-done.5, f32[512,512]{1,0:T(8,128)} %shard_map.51.refs_4_, f32[512,512]{1,0:T(8,128)} %copy-done.6, ...), custom_call_target="tpu_custom_call" | custom-call | flops 3221225472 | bytes 13121536 | tf_op jit(solution)/shard_map/pallas_call | solution.py:63
  (78 shorter events, 21.2 us)
Async XLA Ops:
  2.1 16.2 %collective-permute-start.1 = (f32[1032,128]{1,0:T(8,128)S(1)}, f32[1032,128]{1,0:T(8,128)}, u32[]{:S(2)}, u32[]{:S(2)}) collective-permute-start(f32[1032,128]{1,0:T(8,128)S(1)} %pad_maximum_fusion.refs_17_.refs_15_), channel_id=1, source_target_pairs={{0,4},{1,5},{2,6},{3,7},{4,8},{5,9},{6,10},{7,11},{8,12},{9,13},{1... | collective-permute-start | bytes 1585160 | tf_op jit(solution)/shard_map/ppermute | solution.py:271
  18.4 14.8 %collective-permute-start.2 = (f32[1024,128]{1,0:T(8,128)S(1)}, f32[1024,128]{1,0:T(8,128)S(1)}, u32[]{:S(2)}, u32[]{:S(2)}) collective-permute-start(f32[1024,128]{1,0:T(8,128)S(1)} %slice.39), channel_id=1, source_target_pairs={{0,4},{1,5},{2,6},{3,7},{4,8},{5,9},{6,10},{7,11},{8,12},{9,13},{1... | collective-permute-start | bytes 1572872 | tf_op jit(solution)/shard_map/ppermute | solution.py:271
  24.0 15.3 %collective-permute-start.4 = (f32[1032,128]{1,0:T(8,128)S(1)}, f32[1032,128]{1,0:T(8,128)S(1)}, u32[]{:S(2)}, u32[]{:S(2)}) collective-permute-start(f32[1032,128]{1,0:T(8,128)S(1)} %get-tuple-element.58), channel_id=1, source_target_pairs={{0,1},{1,0},{2,3},{3,2},{4,5},{5,4},{6,7},{7,6},{8,9},{9,8},{10,11... | collective-permute-start | bytes 1585160 | tf_op jit(solution)/shard_map/ppermute | solution.py:268
  33.2 13.8 %collective-permute-start.3 = (f32[1024,128]{1,0:T(8,128)S(1)}, f32[1024,128]{1,0:T(8,128)S(1)}, u32[]{:S(2)}, u32[]{:S(2)}) collective-permute-start(f32[1024,128]{1,0:T(8,128)S(1)} %slice.40), channel_id=1, source_target_pairs={{0,4},{1,5},{2,6},{3,7},{4,8},{5,9},{6,10},{7,11},{8,12},{9,13},{1... | collective-permute-start | bytes 1572872 | tf_op jit(solution)/shard_map/ppermute | solution.py:271
  37.6 15.6 %collective-permute-start.8 = (f32[1032,128]{1,0:T(8,128)S(1)}, f32[1032,128]{1,0:T(8,128)S(1)}, u32[]{:S(2)}, u32[]{:S(2)}) collective-permute-start(f32[1032,128]{1,0:T(8,128)S(1)} %get-tuple-element.85), channel_id=1, source_target_pairs={{0,2},{1,3},{2,0},{3,1},{4,6},{5,7},{6,4},{7,5},{8,10},{9,11},{10,... | collective-permute-start | bytes 1585160 | tf_op jit(solution)/shard_map/ppermute | solution.py:268
  39.3 21.5 %copy-start.7 = (f32[1032,128]{1,0:T(8,128)}, f32[1032,128]{1,0:T(8,128)S(1)}, u32[]{:S(2)}) copy-start(f32[1032,128]{1,0:T(8,128)S(1)} %collective-permute-done.4.refs_2_.refs_7_) | copy-start | bytes 1585156
  39.3 16.0 %collective-permute-start.5 = (f32[1024,128]{1,0:T(8,128)S(1)}, f32[1024,128]{1,0:T(8,128)S(1)}, u32[]{:S(2)}, u32[]{:S(2)}) collective-permute-start(f32[1024,128]{1,0:T(8,128)S(1)} %get-tuple-element.59), channel_id=1, source_target_pairs={{0,1},{1,0},{2,3},{3,2},{4,5},{5,4},{6,7},{7,6},{8,9},{9,8},{10,11... | collective-permute-start | bytes 1572872 | tf_op jit(solution)/shard_map/ppermute | solution.py:268
  47.0 12.8 %collective-permute-start.7 = (f32[1024,128]{1,0:T(8,128)S(1)}, f32[1024,128]{1,0:T(8,128)S(1)}, u32[]{:S(2)}, u32[]{:S(2)}) collective-permute-start(f32[1024,128]{1,0:T(8,128)S(1)} %slice.43), channel_id=1, source_target_pairs={{0,4},{1,5},{2,6},{3,7},{4,8},{5,9},{6,10},{7,11},{8,12},{9,13},{1... | collective-permute-start | bytes 1572872 | tf_op jit(solution)/shard_map/ppermute | solution.py:271
  51.6 14.9 %collective-permute-start.9 = (f32[1024,128]{1,0:T(8,128)S(1)}, f32[1024,128]{1,0:T(8,128)S(1)}, u32[]{:S(2)}, u32[]{:S(2)}) collective-permute-start(f32[1024,128]{1,0:T(8,128)S(1)} %get-tuple-element.83), channel_id=1, source_target_pairs={{0,2},{1,3},{2,0},{3,1},{4,6},{5,7},{6,4},{7,5},{8,10},{9,11},{10,... | collective-permute-start | bytes 1572872 | tf_op jit(solution)/shard_map/ppermute | solution.py:268
  53.2 15.1 %collective-permute-start.14 = (f32[1032,128]{1,0:T(8,128)S(1)}, f32[1032,128]{1,0:T(8,128)}, u32[]{:S(2)}, u32[]{:S(2)}) collective-permute-start(f32[1032,128]{1,0:T(8,128)S(1)} %collective-permute-done.8.refs_6_.refs_13_), channel_id=1, source_target_pairs={{0,1},{1,0},{2,3},{3,2},{4,5},{5,4},{6,7},{7,6},{8,9},{9,8},{10,11... | collective-permute-start | bytes 1585160 | tf_op jit(solution)/shard_map/ppermute | solution.py:268
  54.8 24.7 %collective-permute-start.10 = (f32[1024,128]{1,0:T(8,128)S(1)}, f32[1024,128]{1,0:T(8,128)S(1)}, u32[]{:S(2)}, u32[]{:S(2)}) collective-permute-start(f32[1024,128]{1,0:T(8,128)S(1)} %get-tuple-element.81), channel_id=1, source_target_pairs={{0,2},{1,3},{2,0},{3,1},{4,6},{5,7},{6,4},{7,5},{8,10},{9,11},{10,... | collective-permute-start | bytes 1572872 | tf_op jit(solution)/shard_map/ppermute | solution.py:268
  55.3 24.1 %collective-permute-start.6 = (f32[1024,128]{1,0:T(8,128)S(1)}, f32[1024,128]{1,0:T(8,128)}, u32[]{:S(2)}, u32[]{:S(2)}) collective-permute-start(f32[1024,128]{1,0:T(8,128)S(1)} %get-tuple-element.60), channel_id=1, source_target_pairs={{0,1},{1,0},{2,3},{3,2},{4,5},{5,4},{6,7},{7,6},{8,9},{9,8},{10,11... | collective-permute-start | bytes 1572872 | tf_op jit(solution)/shard_map/ppermute | solution.py:268
  60.8 24.0 %collective-permute-start.11 = (f32[1024,128]{1,0:T(8,128)S(1)}, f32[1024,128]{1,0:T(8,128)S(1)}, u32[]{:S(2)}, u32[]{:S(2)}) collective-permute-start(f32[1024,128]{1,0:T(8,128)S(1)} %get-tuple-element.80), channel_id=1, source_target_pairs={{0,2},{1,3},{2,0},{3,1},{4,6},{5,7},{6,4},{7,5},{8,10},{9,11},{10,... | collective-permute-start | bytes 1572872 | tf_op jit(solution)/shard_map/ppermute | solution.py:268
  66.5 18.3 %copy-start.16 = (f32[1024,128]{1,0:T(8,128)}, f32[1024,128]{1,0:T(8,128)S(1)}, u32[]{:S(2)}) copy-start(f32[1024,128]{1,0:T(8,128)S(1)} %collective-permute-done.9.refs_7_.refs_14_) | copy-start | bytes 1572868
  66.5 42.3 %collective-permute-start = (f32[512,512]{1,0:T(8,128)}, f32[512,512]{1,0:T(8,128)}, u32[]{:S(2)}, u32[]{:S(2)}) collective-permute-start(f32[512,512]{1,0:T(8,128)} %get-tuple-element.50.refs_2_), channel_id=1, source_target_pairs={{0,16},{16,0},{1,17},{17,1},{2,18},{18,2},{3,19},{19,3},{4,20},{20... | collective-permute-start | bytes 3145736 | tf_op jit(solution)/shard_map/ppermute | solution.py:275
  68.3 24.3 %collective-permute-start.15 = (f32[1024,128]{1,0:T(8,128)S(1)}, f32[1024,128]{1,0:T(8,128)S(1)}, u32[]{:S(2)}, u32[]{:S(2)}) collective-permute-start(f32[1024,128]{1,0:T(8,128)S(1)} %collective-permute-done.9.refs_7_.refs_14_), channel_id=1, source_target_pairs={{0,1},{1,0},{2,3},{3,2},{4,5},{5,4},{6,7},{7,6},{8,9},{9,8},{10,11... | collective-permute-start | bytes 1572872 | tf_op jit(solution)/shard_map/ppermute | solution.py:268
  91.9 16.9 %collective-permute-start.12 = (f32[512,512]{1,0:T(8,128)}, f32[512,512]{1,0:T(8,128)}, u32[]{:S(2)}, u32[]{:S(2)}) collective-permute-start(f32[512,512]{1,0:T(8,128)} %get-tuple-element.66.refs_4_), channel_id=1, source_target_pairs={{0,16},{16,0},{1,17},{17,1},{2,18},{18,2},{3,19},{19,3},{4,20},{20... | collective-permute-start | bytes 3145736 | tf_op jit(solution)/shard_map/ppermute | solution.py:275
  92.0 16.8 %collective-permute-start.13 = (f32[512,512]{1,0:T(8,128)}, f32[512,512]{1,0:T(8,128)}, u32[]{:S(2)}, u32[]{:S(2)}) collective-permute-start(f32[512,512]{1,0:T(8,128)} %get-tuple-element.67.refs_6_), channel_id=1, source_target_pairs={{0,16},{16,0},{1,17},{17,1},{2,18},{18,2},{3,19},{19,3},{4,20},{20... | collective-permute-start | bytes 3145736 | tf_op jit(solution)/shard_map/ppermute | solution.py:275
  92.5 27.7 %copy-start.9 = (f32[1024,128]{1,0:T(8,128)}, f32[1024,128]{1,0:T(8,128)S(1)}, u32[]{:S(2)}) copy-start(f32[1024,128]{1,0:T(8,128)S(1)} %collective-permute-done.15.refs_6_.refs_12_) | copy-start | bytes 1572868
  92.5 14.8 %collective-permute-start.17 = (f32[1024,128]{1,0:T(8,128)S(1)}, f32[1024,128]{1,0:T(8,128)S(1)}, u32[]{:S(2)}, u32[]{:S(2)}) collective-permute-start(f32[1024,128]{1,0:T(8,128)S(1)} %copy-done.19), channel_id=1, source_target_pairs={{0,1},{1,0},{2,3},{3,2},{4,5},{5,4},{6,7},{7,6},{8,9},{9,8},{10,11... | collective-permute-start | bytes 1572872 | tf_op jit(solution)/shard_map/ppermute | solution.py:268
  96.6 28.4 %collective-permute-start.16 = (f32[1024,128]{1,0:T(8,128)S(1)}, f32[1024,128]{1,0:T(8,128)S(1)}, u32[]{:S(2)}, u32[]{:S(2)}) collective-permute-start(f32[1024,128]{1,0:T(8,128)S(1)} %copy-done.13), channel_id=1, source_target_pairs={{0,1},{1,0},{2,3},{3,2},{4,5},{5,4},{6,7},{7,6},{8,9},{9,8},{10,11... | collective-permute-start | bytes 1572872 | tf_op jit(solution)/shard_map/ppermute | solution.py:268
  107.4 22.5 %collective-permute-start.19 = (f32[1024,128]{1,0:T(8,128)}, f32[1024,128]{1,0:T(8,128)S(1)}, u32[]{:S(2)}, u32[]{:S(2)}) collective-permute-start(f32[1024,128]{1,0:T(8,128)} %copy-done.17), channel_id=1, source_target_pairs={{0,1},{1,0},{2,3},{3,2},{4,5},{5,4},{6,7},{7,6},{8,9},{9,8},{10,11... | collective-permute-start | bytes 1572872 | tf_op jit(solution)/shard_map/ppermute | solution.py:268
  129.8 6.3 %collective-permute-start.18 = (f32[512,512]{1,0:T(8,128)}, f32[512,512]{1,0:T(8,128)S(1)}, u32[]{:S(2)}, u32[]{:S(2)}) collective-permute-start(f32[512,512]{1,0:T(8,128)} %get-tuple-element.76.refs_2_), channel_id=1, source_target_pairs={{0,16},{16,0},{1,17},{17,1},{2,18},{18,2},{3,19},{19,3},{4,20},{20... | collective-permute-start | bytes 3145736 | tf_op jit(solution)/shard_map/ppermute | solution.py:275
  133.8 3.1 %collective-permute-start.20 = (f32[512,512]{1,0:T(8,128)}, f32[512,512]{1,0:T(8,128)S(1)}, u32[]{:S(2)}, u32[]{:S(2)}) collective-permute-start(f32[512,512]{1,0:T(8,128)} %shard_map.51.refs_4_), channel_id=1, source_target_pairs={{0,16},{16,0},{1,17},{17,1},{2,18},{18,2},{3,19},{19,3},{4,20},{20... | collective-permute-start | bytes 3145736 | tf_op jit(solution)/shard_map/ppermute | solution.py:275
  (17 other events, 124.9 us)
where the time goes:
time: 148 us; the launch traced here: 147 us
  waiting for transfers between devices  54.5 us (37%)
  Pallas kernels  43.4 us (29%)
  starting transfers between devices  36 us (24%)
  local copies, waits for them, and re-layouts  6.62 us (4%)
  between operations  3.57 us (2%)
  other arithmetic  3.4 us (2%)
    pallas_call x7, Pallas kernels, call(): pl.pallas_call(kernel, out_shape=outputs, in_specs=[pl.BlockSpec(memory_s...  43.4 us
    ppermute x12, waiting for transfers between devices, swap(): return lax.ppermute(block, 'occ', [(g, g ^ bit) for g in range(groups)])  30.3 us
    ppermute x4, waiting for transfers between devices, up(): lax.ppermute(block, 'occ', [(g, g + PLANE) for g in range(groups - PLANE)])  23.4 us
    ppermute x4, starting transfers between devices, up(): lax.ppermute(block, 'occ', [(g, g + PLANE) for g in range(groups - PLANE)])  19.3 us
    ppermute x12, starting transfers between devices, swap(): return lax.ppermute(block, 'occ', [(g, g ^ bit) for g in range(groups)])  15.5 us
    unnamed x40, local copies, waits for them, and re-layouts  4.46 us
  transfers between devices with their start and end apart: 21, of which 10 were waited for; matrix products, arithmetic and copies ran while one was open for 3% of the time, Pallas kernels for 23%

commit v1 on v0

--- a/solution.py
+++ b/solution.py
@@ -11,6 +11,7 @@
 SUBLANES = 8
 PLANE = 4
 CHUNKS = 4
+PART_BYTES = 64 * 1024
 VMEM_LIMIT = 60 * 1024 * 1024
 
 
@@ -51,10 +52,14 @@
         self.used = 0
 
     def start(self, source, target):
-        copy = pltpu.make_async_copy(source, target, self.semaphores.at[self.used])
+        semaphore = self.semaphores.at[self.used]
         self.used += 1
-        copy.start()
-        return copy
+        rows = source.shape[0]
+        step = max(min(rows, PART_BYTES * rows // (source.size * source.dtype.itemsize) // 16 * 16), 16)
+        for at in range(0, rows, step):
+            part = pl.ds(at, min(step, rows - at))
+            pltpu.make_async_copy(source.at[part], target.at[part], semaphore).start()
+        return pltpu.make_async_copy(source, target, semaphore)
 
 
 def call(kernel, smem, vmem, anywhere, outputs, out_space, scratch, flops):
@@ -310,7 +315,7 @@
         from_y.append(swap(send_y, 2))
         if at < last:
             from_z.append(up(part(after(own, from_z[at], partial_own), at + 1)))
-        ready = [from_x[at]]
+        ready = [from_x[at], from_y[0]]
         from_d.append(swap(after(from_y[at], from_d[at - 1] if at else from_x[0]), 1))
 
     slot_z, slot_x, slot_y, slot_d = map(slot_of, (from_z, from_x, from_y, from_d))

time: 148 us -> 148 us (level)
  transfers between devices with their start and end apart: 21 -> 21, of which waited for: 10 -> 11; matrix products, arithmetic and copies ran while one was open for 3% -> 3% of each run, Pallas kernels for 23% -> 23%
where the time goes in v1:
time: 148 us; the launch traced here: 147 us
  waiting for transfers between devices  54.7 us (37%)
  Pallas kernels  43.3 us (29%)
  starting transfers between devices  35.8 us (24%)
  local copies, waits for them, and re-layouts  6.62 us (4%)
  between operations  3.57 us (2%)
  other arithmetic  3.4 us (2%)
    pallas_call x7, Pallas kernels, call(): pl.pallas_call(kernel, out_shape=outputs, in_specs=[pl.BlockSpec(memory_s...  43.3 us
    ppermute x12, waiting for transfers between devices, swap(): return lax.ppermute(block, 'occ', [(g, g ^ bit) for g in range(groups)])  30.5 us
    ppermute x4, waiting for transfers between devices, up(): lax.ppermute(block, 'occ', [(g, g + PLANE) for g in range(groups - PLANE)])  23.5 us
    ppermute x4, starting transfers between devices, up(): lax.ppermute(block, 'occ', [(g, g + PLANE) for g in range(groups - PLANE)])  19.3 us
    ppermute x12, starting transfers between devices, swap(): return lax.ppermute(block, 'occ', [(g, g ^ bit) for g in range(groups)])  15.3 us
    unnamed x40, local copies, waits for them, and re-layouts  4.46 us
  transfers between devices with their start and end apart: 21, of which 11 were waited for; matrix products, arithmetic and copies ran while one was open for 3% of the time, Pallas kernels for 23%

profile of v1, /device:TPU:0, one launch (start us, length us, event | category | flops | bytes accessed | tf_op | source)
XLA Modules:
  0.0 147.4 jit_solution(7902795398591750814)
XLA Ops:
  2.1 5.7 %collective-permute-start.1 = (f32[1032,128]{1,0:T(8,128)S(1)}, f32[1032,128]{1,0:T(8,128)}, u32[]{:S(2)}, u32[]{:S(2)}) collective-permute-start(f32[1032,128]{1,0:T(8,128)S(1)} %pad_maximum_fusion.refs_17_.refs_15_), channel_id=1, source_target_pairs={{0,4},{1,5},{2,6},{3,7},{4,8},{5,9},{6,10},{7,11},{8,12},{9,13},{1... | collective-permute-start | bytes 1585160 | tf_op jit(solution)/shard_map/ppermute | solution.py:276
  7.9 4.7 %shard_map.46 = (bf16[4,512,256]{2,1,0:T(8,128)(2,1)}, bf16[4,512,256]{2,1,0:T(8,128)(2,1)}, f32[512,512]{1,0:T(8,128)}) custom-call(f32[4096,128]{1,0:T(8,128)} %bitcast.14), custom_call_target="tpu_custom_call" | custom-call | flops 1610612736 | bytes 5242880 | tf_op jit(solution)/shard_map/pallas_call | solution.py:68
  12.6 5.8 %collective-permute-done.1.refs_2_.refs_9_ = f32[1032,128]{1,0:T(8,128)} collective-permute-done((f32[1032,128]{1,0:T(8,128)S(1)}, f32[1032,128]{1,0:T(8,128)}, u32[]{:S(2)}, u32[]{:S(2)}) %collective-permute-start.1) | collective-permute-done | bytes 528416 | tf_op jit(solution)/shard_map/ppermute | solution.py:276
  18.4 4.5 %collective-permute-start.2 = (f32[1024,128]{1,0:T(8,128)S(1)}, f32[1024,128]{1,0:T(8,128)S(1)}, u32[]{:S(2)}, u32[]{:S(2)}) collective-permute-start(f32[1024,128]{1,0:T(8,128)S(1)} %slice.39), channel_id=1, source_target_pairs={{0,4},{1,5},{2,6},{3,7},{4,8},{5,9},{6,10},{7,11},{8,12},{9,13},{1... | collective-permute-start | bytes 1572872 | tf_op jit(solution)/shard_map/ppermute | solution.py:276
  24.0 1.6 %collective-permute-start.4 = (f32[1032,128]{1,0:T(8,128)S(1)}, f32[1032,128]{1,0:T(8,128)S(1)}, u32[]{:S(2)}, u32[]{:S(2)}) collective-permute-start(f32[1032,128]{1,0:T(8,128)S(1)} %get-tuple-element.58), channel_id=1, source_target_pairs={{0,1},{1,0},{2,3},{3,2},{4,5},{5,4},{6,7},{7,6},{8,9},{9,8},{10,11... | collective-permute-start | bytes 1585160 | tf_op jit(solution)/shard_map/ppermute | solution.py:273
  27.1 6.1 %collective-permute-done.2.refs_3_.refs_10_ = f32[1024,128]{1,0:T(8,128)S(1)} collective-permute-done((f32[1024,128]{1,0:T(8,128)S(1)}, f32[1024,128]{1,0:T(8,128)S(1)}, u32[]{:S(2)}, u32[]{:S(2)}) %collective-permute-start.2) | collective-permute-done | bytes 524320 | tf_op jit(solution)/shard_map/ppermute | solution.py:276
  33.2 4.4 %collective-permute-start.3 = (f32[1024,128]{1,0:T(8,128)S(1)}, f32[1024,128]{1,0:T(8,128)S(1)}, u32[]{:S(2)}, u32[]{:S(2)}) collective-permute-start(f32[1024,128]{1,0:T(8,128)S(1)} %slice.40), channel_id=1, source_target_pairs={{0,4},{1,5},{2,6},{3,7},{4,8},{5,9},{6,10},{7,11},{8,12},{9,13},{1... | collective-permute-start | bytes 1572872 | tf_op jit(solution)/shard_map/ppermute | solution.py:276
  39.3 7.7 %collective-permute-done.3.refs_4_.refs_11_ = f32[1024,128]{1,0:T(8,128)S(1)} collective-permute-done((f32[1024,128]{1,0:T(8,128)S(1)}, f32[1024,128]{1,0:T(8,128)S(1)}, u32[]{:S(2)}, u32[]{:S(2)}) %collective-permute-start.3) | collective-permute-done | bytes 524320 | tf_op jit(solution)/shard_map/ppermute | solution.py:276
  47.0 4.6 %collective-permute-start.8 = (f32[1024,128]{1,0:T(8,128)S(1)}, f32[1024,128]{1,0:T(8,128)S(1)}, u32[]{:S(2)}, u32[]{:S(2)}) collective-permute-start(f32[1024,128]{1,0:T(8,128)S(1)} %slice.43), channel_id=1, source_target_pairs={{0,4},{1,5},{2,6},{3,7},{4,8},{5,9},{6,10},{7,11},{8,12},{9,13},{1... | collective-permute-start | bytes 1572872 | tf_op jit(solution)/shard_map/ppermute | solution.py:276
  51.6 1.6 %collective-permute-start.9 = (f32[1024,128]{1,0:T(8,128)S(1)}, f32[1024,128]{1,0:T(8,128)S(1)}, u32[]{:S(2)}, u32[]{:S(2)}) collective-permute-start(f32[1024,128]{1,0:T(8,128)S(1)} %get-tuple-element.83), channel_id=1, source_target_pairs={{0,2},{1,3},{2,0},{3,1},{4,6},{5,7},{6,4},{7,5},{8,10},{9,11},{10,... | collective-permute-start | bytes 1572872 | tf_op jit(solution)/shard_map/ppermute | solution.py:273
  55.9 4.0 %collective-permute-done.8.refs_5_.refs_12_ = f32[1024,128]{1,0:T(8,128)S(1)} collective-permute-done((f32[1024,128]{1,0:T(8,128)S(1)}, f32[1024,128]{1,0:T(8,128)S(1)}, u32[]{:S(2)}, u32[]{:S(2)}) %collective-permute-start.8) | collective-permute-done | bytes 524320 | tf_op jit(solution)/shard_map/ppermute | solution.py:276
  60.8 1.6 %collective-permute-start.11 = (f32[1024,128]{1,0:T(8,128)S(1)}, f32[1024,128]{1,0:T(8,128)S(1)}, u32[]{:S(2)}, u32[]{:S(2)}) collective-permute-start(f32[1024,128]{1,0:T(8,128)S(1)} %get-tuple-element.80), channel_id=1, source_target_pairs={{0,2},{1,3},{2,0},{3,1},{4,6},{5,7},{6,4},{7,5},{8,10},{9,11},{10,... | collective-permute-start | bytes 1572872 | tf_op jit(solution)/shard_map/ppermute | solution.py:273
  62.4 4.2 %collective-permute-done.9.refs_7_.refs_14_ = f32[1024,128]{1,0:T(8,128)S(1)} collective-permute-done((f32[1024,128]{1,0:T(8,128)S(1)}, f32[1024,128]{1,0:T(8,128)S(1)}, u32[]{:S(2)}, u32[]{:S(2)}) %collective-permute-start.9) | collective-permute-done | bytes 524320 | tf_op jit(solution)/shard_map/ppermute | solution.py:273
  66.5 1.7 %collective-permute-done.14.refs_5_.refs_11_ = f32[1032,128]{1,0:T(8,128)} collective-permute-done((f32[1032,128]{1,0:T(8,128)S(1)}, f32[1032,128]{1,0:T(8,128)}, u32[]{:S(2)}, u32[]{:S(2)}) %collective-permute-start.14) | collective-permute-done | bytes 528416 | tf_op jit(solution)/shard_map/ppermute | solution.py:273
  69.7 9.7 %collective-permute-done.7.refs_4_.refs_9_ = f32[1024,128]{1,0:T(8,128)} collective-permute-done((f32[1024,128]{1,0:T(8,128)S(1)}, f32[1024,128]{1,0:T(8,128)}, u32[]{:S(2)}, u32[]{:S(2)}) %collective-permute-start.7) | collective-permute-done | bytes 524320 | tf_op jit(solution)/shard_map/ppermute | solution.py:273
  80.3 4.5 %collective-permute-done.11.refs_9_.refs_16_ = f32[1024,128]{1,0:T(8,128)S(1)} collective-permute-done((f32[1024,128]{1,0:T(8,128)S(1)}, f32[1024,128]{1,0:T(8,128)S(1)}, u32[]{:S(2)}, u32[]{:S(2)}) %collective-permute-start.11) | collective-permute-done | bytes 524320 | tf_op jit(solution)/shard_map/ppermute | solution.py:273
  85.6 6.3 %shard_map.47 = (f32[512,512]{1,0:T(8,128)}, f32[512,512]{1,0:T(8,128)}) custom-call(bf16[4,512,256]{2,1,0:T(8,128)(2,1)} %get-tuple-element.68.refs_0_, bf16[4,512,256]{2,1,0:T(8,128)(2,1)} %get-tuple-element.69.refs_1_, f32[1032,128]{1,0:T(8,128)} %collective-permute-done.1.refs_2_.refs_9_, f32[1024,128]{1,0:T(8,128)} %copy-done.10, ...), custom_call_target="tpu_custom_call" | custom-call | flops 3221225472 | bytes 8396800 | tf_op jit(solution)/shard_map/pallas_call | solution.py:68
  92.5 1.6 %collective-permute-start.17 = (f32[1024,128]{1,0:T(8,128)S(1)}, f32[1024,128]{1,0:T(8,128)S(1)}, u32[]{:S(2)}, u32[]{:S(2)}) collective-permute-start(f32[1024,128]{1,0:T(8,128)S(1)} %copy-done.19), channel_id=1, source_target_pairs={{0,1},{1,0},{2,3},{3,2},{4,5},{5,4},{6,7},{7,6},{8,9},{9,8},{10,11... | collective-permute-start | bytes 1572872 | tf_op jit(solution)/shard_map/ppermute | solution.py:273
  97.2 10.2 %collective-permute-done.17.refs_5_.refs_13_ = f32[1024,128]{1,0:T(8,128)S(1)} collective-permute-done((f32[1024,128]{1,0:T(8,128)S(1)}, f32[1024,128]{1,0:T(8,128)S(1)}, u32[]{:S(2)}, u32[]{:S(2)}) %collective-permute-start.17) | collective-permute-done | bytes 524320 | tf_op jit(solution)/shard_map/ppermute | solution.py:273
  108.9 11.3 %shard_map.48.refs_6_ = f32[4096,128]{1,0:T(8,128)} custom-call(f32[3]{0:T(128)} %pad_maximum_fusion.2.refs_0_, f32[1,512]{1,0:T(1,128)} %bitcast.24, f32[512,512]{1,0:T(8,128)} %get-tuple-element.50.refs_2_, f32[512,512]{1,0:T(8,128)} %collective-permute-done.refs_3_, f32[512,512]{1,0:T(8,128)} %get-tuple-element.66.refs_4_, ...), custom_call_target="tpu_custom_call" | custom-call | flops 4831838208 | bytes 15218688 | tf_op jit(solution)/shard_map/pallas_call | solution.py:68
  120.2 4.8 %shard_map.49 = (f32[512,512]{1,0:T(8,128)}, f32[512,512]{1,0:T(8,128)}) custom-call(bf16[4,512,256]{2,1,0:T(8,128)(2,1)} %get-tuple-element.68.refs_0_, bf16[4,512,256]{2,1,0:T(8,128)(2,1)} %get-tuple-element.69.refs_1_, f32[1032,128]{1,0:T(8,128)} %copy-done.7, f32[1024,128]{1,0:T(8,128)} %copy-done.8, f32[1024,128]{1,0:T(8,128)} %collective-permute-done.7.refs_4_.refs_9_, ...), custom_call_target="tpu_custom_call" | custom-call | flops 2013265920 | bytes 6823936 | tf_op jit(solution)/shard_map/pallas_call | solution.py:68
  125.9 3.9 %shard_map.50 = (f32[512,512]{1,0:T(8,128)}, f32[512,512]{1,0:T(8,128)}) custom-call(bf16[4,512,256]{2,1,0:T(8,128)(2,1)} %get-tuple-element.68.refs_0_, bf16[4,512,256]{2,1,0:T(8,128)(2,1)} %get-tuple-element.69.refs_1_, f32[512,512]{1,0:T(8,128)} %get-tuple-element.72.refs_2_, f32[512,512]{1,0:T(8,128)} %get-tuple-element.73.refs_3_, ...), custom_call_target="tpu_custom_call" | custom-call | flops 805306368 | bytes 7340032 | tf_op jit(solution)/shard_map/pallas_call | solution.py:68
  130.7 2.9 %shard_map.51.refs_4_ = f32[512,512]{1,0:T(8,128)} custom-call(bf16[4,512,256]{2,1,0:T(8,128)(2,1)} %get-tuple-element.68.refs_0_, bf16[4,512,256]{2,1,0:T(8,128)(2,1)} %get-tuple-element.69.refs_1_, f32[512,512]{1,0:T(8,128)} %get-tuple-element.77.refs_2_, f32[1024,128]{1,0:T(8,128)} %copy-done.4), custom_call_target="tpu_custom_call" | custom-call | flops 402653184 | bytes 4718592 | tf_op jit(solution)/shard_map/pallas_call | solution.py:68
  137.9 9.3 %shard_map.52 = f32[4096,128]{1,0:T(8,128)} custom-call(f32[2]{0:T(128)} %pad_maximum_fusion.1.refs_0_, f32[1,512]{1,0:T(1,128)} %bitcast.25, f32[512,512]{1,0:T(8,128)} %get-tuple-element.76.refs_2_, f32[512,512]{1,0:T(8,128)} %copy-done.5, f32[512,512]{1,0:T(8,128)} %shard_map.51.refs_4_, f32[512,512]{1,0:T(8,128)} %copy-done.6, ...), custom_call_target="tpu_custom_call" | custom-call | flops 3221225472 | bytes 13121536 | tf_op jit(solution)/shard_map/pallas_call | solution.py:68
  (78 shorter events, 21.2 us)
Async XLA Ops:
  2.1 16.2 %collective-permute-start.1 = (f32[1032,128]{1,0:T(8,128)S(1)}, f32[1032,128]{1,0:T(8,128)}, u32[]{:S(2)}, u32[]{:S(2)}) collective-permute-start(f32[1032,128]{1,0:T(8,128)S(1)} %pad_maximum_fusion.refs_17_.refs_15_), channel_id=1, source_target_pairs={{0,4},{1,5},{2,6},{3,7},{4,8},{5,9},{6,10},{7,11},{8,12},{9,13},{1... | collective-permute-start | bytes 1585160 | tf_op jit(solution)/shard_map/ppermute | solution.py:276
  18.4 14.8 %collective-permute-start.2 = (f32[1024,128]{1,0:T(8,128)S(1)}, f32[1024,128]{1,0:T(8,128)S(1)}, u32[]{:S(2)}, u32[]{:S(2)}) collective-permute-start(f32[1024,128]{1,0:T(8,128)S(1)} %slice.39), channel_id=1, source_target_pairs={{0,4},{1,5},{2,6},{3,7},{4,8},{5,9},{6,10},{7,11},{8,12},{9,13},{1... | collective-permute-start | bytes 1572872 | tf_op jit(solution)/shard_map/ppermute | solution.py:276
  24.0 13.7 %collective-permute-start.4 = (f32[1032,128]{1,0:T(8,128)S(1)}, f32[1032,128]{1,0:T(8,128)S(1)}, u32[]{:S(2)}, u32[]{:S(2)}) collective-permute-start(f32[1032,128]{1,0:T(8,128)S(1)} %get-tuple-element.58), channel_id=1, source_target_pairs={{0,1},{1,0},{2,3},{3,2},{4,5},{5,4},{6,7},{7,6},{8,9},{9,8},{10,11... | collective-permute-start | bytes 1585160 | tf_op jit(solution)/shard_map/ppermute | solution.py:273
  25.6 12.3 %collective-permute-start.5 = (f32[1032,128]{1,0:T(8,128)S(1)}, f32[1032,128]{1,0:T(8,128)S(1)}, u32[]{:S(2)}, u32[]{:S(2)}) collective-permute-start(f32[1032,128]{1,0:T(8,128)S(1)} %get-tuple-element.85), channel_id=1, source_target_pairs={{0,2},{1,3},{2,0},{3,1},{4,6},{5,7},{6,4},{7,5},{8,10},{9,11},{10,... | collective-permute-start | bytes 1585160 | tf_op jit(solution)/shard_map/ppermute | solution.py:273
  33.2 13.8 %collective-permute-start.3 = (f32[1024,128]{1,0:T(8,128)S(1)}, f32[1024,128]{1,0:T(8,128)S(1)}, u32[]{:S(2)}, u32[]{:S(2)}) collective-permute-start(f32[1024,128]{1,0:T(8,128)S(1)} %slice.40), channel_id=1, source_target_pairs={{0,4},{1,5},{2,6},{3,7},{4,8},{5,9},{6,10},{7,11},{8,12},{9,13},{1... | collective-permute-start | bytes 1572872 | tf_op jit(solution)/shard_map/ppermute | solution.py:276
  37.7 23.1 %copy-start.7 = (f32[1032,128]{1,0:T(8,128)}, f32[1032,128]{1,0:T(8,128)S(1)}, u32[]{:S(2)}) copy-start(f32[1032,128]{1,0:T(8,128)S(1)} %collective-permute-done.4.refs_2_.refs_7_) | copy-start | bytes 1585156
  37.9 22.9 %copy-start.15 = (f32[1032,128]{1,0:T(8,128)}, f32[1032,128]{1,0:T(8,128)S(1)}, u32[]{:S(2)}) copy-start(f32[1032,128]{1,0:T(8,128)S(1)} %collective-permute-done.5.refs_6_.refs_13_) | copy-start | bytes 1585156
  37.9 17.4 %collective-permute-start.6 = (f32[1024,128]{1,0:T(8,128)S(1)}, f32[1024,128]{1,0:T(8,128)S(1)}, u32[]{:S(2)}, u32[]{:S(2)}) collective-permute-start(f32[1024,128]{1,0:T(8,128)S(1)} %get-tuple-element.59), channel_id=1, source_target_pairs={{0,1},{1,0},{2,3},{3,2},{4,5},{5,4},{6,7},{7,6},{8,9},{9,8},{10,11... | collective-permute-start | bytes 1572872 | tf_op jit(solution)/shard_map/ppermute | solution.py:273
  47.0 12.8 %collective-permute-start.8 = (f32[1024,128]{1,0:T(8,128)S(1)}, f32[1024,128]{1,0:T(8,128)S(1)}, u32[]{:S(2)}, u32[]{:S(2)}) collective-permute-start(f32[1024,128]{1,0:T(8,128)S(1)} %slice.43), channel_id=1, source_target_pairs={{0,4},{1,5},{2,6},{3,7},{4,8},{5,9},{6,10},{7,11},{8,12},{9,13},{1... | collective-permute-start | bytes 1572872 | tf_op jit(solution)/shard_map/ppermute | solution.py:276
  51.6 14.9 %collective-permute-start.9 = (f32[1024,128]{1,0:T(8,128)S(1)}, f32[1024,128]{1,0:T(8,128)S(1)}, u32[]{:S(2)}, u32[]{:S(2)}) collective-permute-start(f32[1024,128]{1,0:T(8,128)S(1)} %get-tuple-element.83), channel_id=1, source_target_pairs={{0,2},{1,3},{2,0},{3,1},{4,6},{5,7},{6,4},{7,5},{8,10},{9,11},{10,... | collective-permute-start | bytes 1572872 | tf_op jit(solution)/shard_map/ppermute | solution.py:273
  53.2 15.1 %collective-permute-start.14 = (f32[1032,128]{1,0:T(8,128)S(1)}, f32[1032,128]{1,0:T(8,128)}, u32[]{:S(2)}, u32[]{:S(2)}) collective-permute-start(f32[1032,128]{1,0:T(8,128)S(1)} %collective-permute-done.5.refs_6_.refs_13_), channel_id=1, source_target_pairs={{0,1},{1,0},{2,3},{3,2},{4,5},{5,4},{6,7},{7,6},{8,9},{9,8},{10,11... | collective-permute-start | bytes 1585160 | tf_op jit(solution)/shard_map/ppermute | solution.py:273
  54.8 24.7 %collective-permute-start.10 = (f32[1024,128]{1,0:T(8,128)S(1)}, f32[1024,128]{1,0:T(8,128)S(1)}, u32[]{:S(2)}, u32[]{:S(2)}) collective-permute-start(f32[1024,128]{1,0:T(8,128)S(1)} %get-tuple-element.81), channel_id=1, source_target_pairs={{0,2},{1,3},{2,0},{3,1},{4,6},{5,7},{6,4},{7,5},{8,10},{9,11},{10,... | collective-permute-start | bytes 1572872 | tf_op jit(solution)/shard_map/ppermute | solution.py:273
  55.3 24.1 %collective-permute-start.7 = (f32[1024,128]{1,0:T(8,128)S(1)}, f32[1024,128]{1,0:T(8,128)}, u32[]{:S(2)}, u32[]{:S(2)}) collective-permute-start(f32[1024,128]{1,0:T(8,128)S(1)} %get-tuple-element.60), channel_id=1, source_target_pairs={{0,1},{1,0},{2,3},{3,2},{4,5},{5,4},{6,7},{7,6},{8,9},{9,8},{10,11... | collective-permute-start | bytes 1572872 | tf_op jit(solution)/shard_map/ppermute | solution.py:273
  60.8 24.0 %collective-permute-start.11 = (f32[1024,128]{1,0:T(8,128)S(1)}, f32[1024,128]{1,0:T(8,128)S(1)}, u32[]{:S(2)}, u32[]{:S(2)}) collective-permute-start(f32[1024,128]{1,0:T(8,128)S(1)} %get-tuple-element.80), channel_id=1, source_target_pairs={{0,2},{1,3},{2,0},{3,1},{4,6},{5,7},{6,4},{7,5},{8,10},{9,11},{10,... | collective-permute-start | bytes 1572872 | tf_op jit(solution)/shard_map/ppermute | solution.py:273
  66.5 42.3 %collective-permute-start = (f32[512,512]{1,0:T(8,128)}, f32[512,512]{1,0:T(8,128)}, u32[]{:S(2)}, u32[]{:S(2)}) collective-permute-start(f32[512,512]{1,0:T(8,128)} %get-tuple-element.50.refs_2_), channel_id=1, source_target_pairs={{0,16},{16,0},{1,17},{17,1},{2,18},{18,2},{3,19},{19,3},{4,20},{20... | collective-permute-start | bytes 3145736 | tf_op jit(solution)/shard_map/ppermute | solution.py:280
  68.2 24.3 %collective-permute-start.15 = (f32[1024,128]{1,0:T(8,128)S(1)}, f32[1024,128]{1,0:T(8,128)S(1)}, u32[]{:S(2)}, u32[]{:S(2)}) collective-permute-start(f32[1024,128]{1,0:T(8,128)S(1)} %collective-permute-done.9.refs_7_.refs_14_), channel_id=1, source_target_pairs={{0,1},{1,0},{2,3},{3,2},{4,5},{5,4},{6,7},{7,6},{8,9},{9,8},{10,11... | collective-permute-start | bytes 1572872 | tf_op jit(solution)/shard_map/ppermute | solution.py:273
  92.0 16.9 %collective-permute-start.12 = (f32[512,512]{1,0:T(8,128)}, f32[512,512]{1,0:T(8,128)}, u32[]{:S(2)}, u32[]{:S(2)}) collective-permute-start(f32[512,512]{1,0:T(8,128)} %get-tuple-element.66.refs_4_), channel_id=1, source_target_pairs={{0,16},{16,0},{1,17},{17,1},{2,18},{18,2},{3,19},{19,3},{4,20},{20... | collective-permute-start | bytes 3145736 | tf_op jit(solution)/shard_map/ppermute | solution.py:280
  92.0 16.8 %collective-permute-start.13 = (f32[512,512]{1,0:T(8,128)}, f32[512,512]{1,0:T(8,128)}, u32[]{:S(2)}, u32[]{:S(2)}) collective-permute-start(f32[512,512]{1,0:T(8,128)} %get-tuple-element.67.refs_6_), channel_id=1, source_target_pairs={{0,16},{16,0},{1,17},{17,1},{2,18},{18,2},{3,19},{19,3},{4,20},{20... | collective-permute-start | bytes 3145736 | tf_op jit(solution)/shard_map/ppermute | solution.py:280
  92.5 27.7 %copy-start.9 = (f32[1024,128]{1,0:T(8,128)}, f32[1024,128]{1,0:T(8,128)S(1)}, u32[]{:S(2)}) copy-start(f32[1024,128]{1,0:T(8,128)S(1)} %collective-permute-done.15.refs_6_.refs_12_) | copy-start | bytes 1572868
  92.5 14.8 %collective-permute-start.17 = (f32[1024,128]{1,0:T(8,128)S(1)}, f32[1024,128]{1,0:T(8,128)S(1)}, u32[]{:S(2)}, u32[]{:S(2)}) collective-permute-start(f32[1024,128]{1,0:T(8,128)S(1)} %copy-done.19), channel_id=1, source_target_pairs={{0,1},{1,0},{2,3},{3,2},{4,5},{5,4},{6,7},{7,6},{8,9},{9,8},{10,11... | collective-permute-start | bytes 1572872 | tf_op jit(solution)/shard_map/ppermute | solution.py:273
  96.7 28.5 %collective-permute-start.16 = (f32[1024,128]{1,0:T(8,128)S(1)}, f32[1024,128]{1,0:T(8,128)S(1)}, u32[]{:S(2)}, u32[]{:S(2)}) collective-permute-start(f32[1024,128]{1,0:T(8,128)S(1)} %copy-done.13), channel_id=1, source_target_pairs={{0,1},{1,0},{2,3},{3,2},{4,5},{5,4},{6,7},{7,6},{8,9},{9,8},{10,11... | collective-permute-start | bytes 1572872 | tf_op jit(solution)/shard_map/ppermute | solution.py:273
  107.4 22.5 %collective-permute-start.19 = (f32[1024,128]{1,0:T(8,128)}, f32[1024,128]{1,0:T(8,128)S(1)}, u32[]{:S(2)}, u32[]{:S(2)}) collective-permute-start(f32[1024,128]{1,0:T(8,128)} %copy-done.17), channel_id=1, source_target_pairs={{0,1},{1,0},{2,3},{3,2},{4,5},{5,4},{6,7},{7,6},{8,9},{9,8},{10,11... | collective-permute-start | bytes 1572872 | tf_op jit(solution)/shard_map/ppermute | solution.py:273
  129.8 6.2 %collective-permute-start.18 = (f32[512,512]{1,0:T(8,128)}, f32[512,512]{1,0:T(8,128)S(1)}, u32[]{:S(2)}, u32[]{:S(2)}) collective-permute-start(f32[512,512]{1,0:T(8,128)} %get-tuple-element.76.refs_2_), channel_id=1, source_target_pairs={{0,16},{16,0},{1,17},{17,1},{2,18},{18,2},{3,19},{19,3},{4,20},{20... | collective-permute-start | bytes 3145736 | tf_op jit(solution)/shard_map/ppermute | solution.py:280
  133.7 3.1 %collective-permute-start.20 = (f32[512,512]{1,0:T(8,128)}, f32[512,512]{1,0:T(8,128)S(1)}, u32[]{:S(2)}, u32[]{:S(2)}) collective-permute-start(f32[512,512]{1,0:T(8,128)} %shard_map.51.refs_4_), channel_id=1, source_target_pairs={{0,16},{16,0},{1,17},{17,1},{2,18},{18,2},{3,19},{19,3},{4,20},{20... | collective-permute-start | bytes 3145736 | tf_op jit(solution)/shard_map/ppermute | solution.py:280
  (17 other events, 135.7 us)
